TPU v7x, 32 devices: a whole 2x2x4 slice. The times are simulated.
32 devices in a mesh: cand: 4 (over z), slab: 8 (over y, x, core).
Axes of the slice: x: 2, y: 2, z: 4, core: 2. Of those that a mesh axis runs over, the one named last changes fastest.
Arguments:
- velocity: float32 [3, 32, 32, 128], P(None, 'slab'), may hold values from -6 to 6
- stress: float32 [6, 32, 32, 128], P(None, 'slab'), may hold values from -6 to 6
- lame_lambda: bfloat16 [32, 32, 128], P('slab'), may hold values from 0.5 to 1.5
- shear_modulus: bfloat16 [32, 32, 128], P('slab'), may hold values from 0.29882812 to 1
- buoyancy: bfloat16 [32, 32, 128], P('slab'), may hold values from 0.5 to 1.5
- surface: float32 [8, 6, 32, 32], P(None, None, 'slab', 'cand'), may hold values from -6 to 6
- block_owner: int32 [4], replicated, may hold values from 0 to 3, each once
- candidates: float32 [16, 3], replicated, may hold values from 0.7 to 1.4
- candidate_of_group: int32 [16], replicated, may hold values from 0 to 15, each once
Outputs:
- velocity_out: float32 [4, 3, 32, 32, 128], P('cand', None, 'slab')
- stress_out: float32 [4, 6, 32, 32, 128], P('cand', None, 'slab')
Inputs may be any that keep to these rules, and one draw needn't show every extreme that they name: `block_owner`: each slot holds exactly one block. `candidate_of_group`: each candidate appears exactly once.
All inputs are finite; a program needn't handle non-finite values.
Results may differ from a plain program's by a relative error of at most 0.0003.
Values sent between devices are 32-bit elements; how exact they have to be, the bound alone decides.
A program may use at most 64 MiB of HBM per device.

v0:
```python
import jax
import jax.numpy as jnp
from jax import lax
from jax.sharding import PartitionSpec as P

DT = 0.15


def from_root(array, axis, root):
    mine = lax.axis_index(axis) == root
    return lax.psum(jnp.where(mine, array, jnp.zeros_like(array)), axis)


def from_behind(value, axis, steps):
    count = lax.axis_size(axis)
    first, last = (max(0, -steps), min(count, count - steps))
    return lax.ppermute(value, axis, [(source, source + steps) for source in range(first, last)])


def minus_x(field, lower):
    return field - jnp.concatenate([lower[None], field[:-1]], axis=0)


def plus_x(field, upper):
    return jnp.concatenate([field[1:], upper[None]], axis=0) - field


def minus_y(field):
    edge = jnp.zeros_like(field[..., :1, :])
    return field - jnp.concatenate([edge, field[..., :-1, :]], axis=-2)


def plus_y(field):
    edge = jnp.zeros_like(field[..., :1, :])
    return jnp.concatenate([field[..., 1:, :], edge], axis=-2) - field


def minus_z(field):
    edge = jnp.zeros_like(field[..., :1])
    return field - jnp.concatenate([edge, field[..., :-1]], axis=-1)


def plus_z(field):
    edge = jnp.zeros_like(field[..., :1])
    return jnp.concatenate([field[..., 1:], edge], axis=-1) - field


def advance_velocity(vel, sig, lower, buoy, inject, zmask):
    acc_x = (
        minus_x(sig[0], lower[0]) + minus_y(sig[3]) + minus_z(sig[4]) + inject[0][..., None] * zmask
    )
    acc_y = (
        minus_x(sig[3], lower[1]) + minus_y(sig[1]) + minus_z(sig[5]) + inject[1][..., None] * zmask
    )
    acc_z = (
        minus_x(sig[4], lower[2]) + minus_y(sig[5]) + minus_z(sig[2]) + inject[2][..., None] * zmask
    )
    return vel + DT * buoy * jnp.stack([acc_x, acc_y, acc_z])


def advance_stress(sig, vel, upper, lam, shear, inject, zmask):
    strain_xx = plus_x(vel[0], upper[0])
    strain_yy = plus_y(vel[1])
    strain_zz = plus_z(vel[2])
    spread = strain_xx + strain_yy + strain_zz
    new_xx = sig[0] + DT * (lam * spread + 2.0 * shear * strain_xx)
    new_yy = sig[1] + DT * (lam * spread + 2.0 * shear * strain_yy)
    new_zz = sig[2] + DT * (
        lam * spread
        + 2.0 * shear * strain_zz
        + (lam + 2.0 * shear) * (inject[2][..., None] * zmask)
    )
    new_xy = sig[3] + DT * shear * (plus_y(vel[0]) + plus_x(vel[1], upper[1]))
    new_xz = sig[4] + DT * shear * (
        plus_z(vel[0]) + plus_x(vel[2], upper[2]) + inject[0][..., None] * zmask
    )
    new_yz = sig[5] + DT * shear * (plus_z(vel[1]) + plus_y(vel[2]) + inject[1][..., None] * zmask)
    return jnp.stack([new_xx, new_yy, new_zz, new_xy, new_xz, new_yz])


def deliver(surface, block_owner):
    blocks = block_owner.shape[0]
    columns = surface.shape[3]
    start_plane = jnp.zeros(surface.shape[:3] + (columns * blocks,), jnp.float32)

    def place(index, plane):
        piece = from_root(surface, "cand", block_owner[index])
        return lax.dynamic_update_slice_in_dim(plane, piece, index * columns, 3)

    return lax.fori_loop(0, blocks, place, start_plane)


def body(
    velocity,
    stress,
    lame_lambda,
    shear_modulus,
    buoyancy,
    surface,
    block_owner,
    candidates,
    candidate_of_group,
):
    plane = deliver(surface, block_owner)
    group = lax.axis_index("cand")
    row = candidates[candidate_of_group[group]]
    depth_z = velocity.shape[-1]
    width = velocity.shape[-2]
    planes = velocity.shape[1]
    steps = plane.shape[0]
    levels = jnp.arange(depth_z)
    zone = (levels >= depth_z // 2).astype(jnp.float32)
    zmask = (levels == depth_z // 8).astype(jnp.float32)
    lam = lame_lambda.astype(jnp.float32) * (1.0 + (row[0] - 1.0) * zone)
    shear = shear_modulus.astype(jnp.float32) * (1.0 + (row[1] - 1.0) * zone)
    buoy = buoyancy.astype(jnp.float32) * (1.0 + (row[2] - 1.0) * zone)
    margin = 1
    moduli = jnp.stack([lam, shear, buoy])
    upper_size = 3 * margin * width * depth_z
    bottom_pack = jnp.concatenate(
        [moduli[:, :margin].reshape(-1), plane[:, :, :margin].reshape(-1)]
    )
    from_above = from_behind(bottom_pack, "slab", -1)
    zero_moduli = jnp.zeros((3, 1, width, depth_z), jnp.float32)
    zero_rows = jnp.zeros((steps, 6, 1, width), jnp.float32)
    moduli_ext = jnp.concatenate(
        [zero_moduli, moduli, from_above[:upper_size].reshape(3, margin, width, depth_z)], axis=1
    )
    plane_ext = jnp.concatenate(
        [zero_rows, plane, from_above[upper_size:].reshape(steps, 6, margin, width)], axis=2
    )
    lam_ext, shear_ext, buoy_ext = (moduli_ext[0], moduli_ext[1], moduli_ext[2])
    border = jnp.zeros((3, width, depth_z), jnp.float32)
    vel, sig = (velocity, stress)
    for turn in range(steps // margin):
        state = jnp.concatenate([vel, sig])
        low_state = from_behind(state[:, planes - margin :], "slab", 1)
        high_state = from_behind(state[:, :margin], "slab", -1)
        widened = jnp.concatenate([low_state, state, high_state], axis=1)
        vel_ext, sig_ext = (widened[:3], widened[3:])
        step = turn * margin
        vel_ext = advance_velocity(vel_ext, sig_ext, border, buoy_ext, plane_ext[step, :3], zmask)
        sig_ext = advance_stress(
            sig_ext, vel_ext, border, lam_ext, shear_ext, plane_ext[step, 3:], zmask
        )
        vel = vel_ext[:, margin : margin + planes]
        sig = sig_ext[:, margin : margin + planes]
    return (vel[None], sig[None])


def solution(mesh):
    in_specs = (
        P(None, "slab", None, None),
        P(None, "slab", None, None),
        P("slab", None, None),
        P("slab", None, None),
        P("slab", None, None),
        P(None, None, "slab", "cand"),
        P(),
        P(),
        P(),
    )
    out_specs = (P("cand", None, "slab", None, None), P("cand", None, "slab", None, None))
    return jax.shard_map(body, mesh=mesh, in_specs=in_specs, out_specs=out_specs, check_vma=False)
```

profile of v0, /device:TPU:3, one launch (start us, length us, event | category | flops | bytes accessed | tf_op | source)
XLA Modules:
  0.0 202.4 jit_solution(7250917588369917624)
XLA Ops:
  7.2 86.4 %while.13 = (s32[]{:T(128)}, f32[8,6,4,32]{3,2,1,0:T(4,128)S(1)}, s32[4]{0:T(128)S(1)}, f32[8,6,4,8]{3,2,1,0:T(4,128)S(1)}, s32[]{:T(128)}, /*index=5*/u32[]{:T(128)}, s32[]{:T(128)}, s32[]{:T(128)}, s32[]{:T(128)}) while((s32[]{:T(128)}, f32[8,6,4,32]{3,2,1,0:T(4,128)S(1)}, s32[4]{0:T(128)S(1)}, f32[8,6,4,8]{3,2,1,0:T(4,128)S(1)}, s32[]{:T(128)}, ...), condition=%wide.region_2.3_spmd, body=%wide.region_0.2_spmd.sunk | while | flops 3082 | bytes 37061 | solution.py:90
  8.5 16.7 %psum.12 = f32[8,6,4,8]{3,2,1,0:T(4,128)S(1)} all-reduce(f32[8,6,4,8]{3,2,1,0:T(4,128)S(1)} %broadcast_select_fusion.2), channel_id=1, replica_groups=mesh['cand'=4,'slab'=8] {'cand'}, use_global_device_ids=true, to_apply=%region_1.1 | all-reduce | flops 1536 | bytes 12288 | tf_op jit(solution)/shard_map/while/body/eval_jaxpr/psum | solution.py:11
  27.3 13.8 %psum.12 = f32[8,6,4,8]{3,2,1,0:T(4,128)S(1)} all-reduce(f32[8,6,4,8]{3,2,1,0:T(4,128)S(1)} %broadcast_select_fusion.2), channel_id=1, replica_groups=mesh['cand'=4,'slab'=8] {'cand'}, use_global_device_ids=true, to_apply=%region_1.1 | all-reduce | flops 1536 | bytes 12288 | tf_op jit(solution)/shard_map/while/body/eval_jaxpr/psum | solution.py:11
  41.1 7.2 %dynamic_update_slice.8 = f32[8,6,4,32]{3,2,1,0:T(4,128)S(1)} dynamic-update-slice(f32[8,6,4,32]{3,2,1,0:T(4,128)S(1)} %get-tuple-element.364, f32[8,6,4,8]{3,2,1,0:T(4,128)S(1)} %psum.12, s32[]{:T(128)} %constant.83.clone.1..sunk, s32[]{:T(128)} %constant.83.clone.1..sunk, s32[]{:T(128)} %constant.83.clone.1..sunk, s32[]{:T(128)S(6)} %select_n.43) | dynamic-update-slice | bytes 12292 | tf_op jit(solution)/shard_map/while/body/eval_jaxpr/dynamic_update_slice | solution.py:88
  49.6 14.7 %psum.12 = f32[8,6,4,8]{3,2,1,0:T(4,128)S(1)} all-reduce(f32[8,6,4,8]{3,2,1,0:T(4,128)S(1)} %broadcast_select_fusion.2), channel_id=1, replica_groups=mesh['cand'=4,'slab'=8] {'cand'}, use_global_device_ids=true, to_apply=%region_1.1 | all-reduce | flops 1536 | bytes 12288 | tf_op jit(solution)/shard_map/while/body/eval_jaxpr/psum | solution.py:11
  64.3 7.2 %dynamic_update_slice.8 = f32[8,6,4,32]{3,2,1,0:T(4,128)S(1)} dynamic-update-slice(f32[8,6,4,32]{3,2,1,0:T(4,128)S(1)} %get-tuple-element.364, f32[8,6,4,8]{3,2,1,0:T(4,128)S(1)} %psum.12, s32[]{:T(128)} %constant.83.clone.1..sunk, s32[]{:T(128)} %constant.83.clone.1..sunk, s32[]{:T(128)} %constant.83.clone.1..sunk, s32[]{:T(128)S(6)} %select_n.43) | dynamic-update-slice | bytes 12292 | tf_op jit(solution)/shard_map/while/body/eval_jaxpr/dynamic_update_slice | solution.py:88
  72.8 13.6 %psum.12 = f32[8,6,4,8]{3,2,1,0:T(4,128)S(1)} all-reduce(f32[8,6,4,8]{3,2,1,0:T(4,128)S(1)} %broadcast_select_fusion.2), channel_id=1, replica_groups=mesh['cand'=4,'slab'=8] {'cand'}, use_global_device_ids=true, to_apply=%region_1.1 | all-reduce | flops 1536 | bytes 12288 | tf_op jit(solution)/shard_map/while/body/eval_jaxpr/psum | solution.py:11
  86.4 7.2 %dynamic_update_slice.8 = f32[8,6,4,32]{3,2,1,0:T(4,128)S(1)} dynamic-update-slice(f32[8,6,4,32]{3,2,1,0:T(4,128)S(1)} %get-tuple-element.364, f32[8,6,4,8]{3,2,1,0:T(4,128)S(1)} %psum.12, s32[]{:T(128)} %constant.83.clone.1..sunk, s32[]{:T(128)} %constant.83.clone.1..sunk, s32[]{:T(128)} %constant.83.clone.1..sunk, s32[]{:T(128)S(6)} %select_n.43) | dynamic-update-slice | bytes 12292 | tf_op jit(solution)/shard_map/while/body/eval_jaxpr/dynamic_update_slice | solution.py:88
  95.3 17.8 %collective-permute-start.2 = (f32[13824]{0:T(1024)S(1)}, f32[13824]{0:T(1024)S(1)}, u32[]{:S(2)}, u32[]{:S(2)}) collective-permute-start(f32[13824]{0:T(1024)S(1)} %pad_maximum_fusion.39), channel_id=1, source_target_pairs={{1,0},{2,1},{3,2},{4,3},{5,4},{6,5},{7,6},{9,8},{10,9},{11,10},{12... | collective-permute-start | bytes 165896 | tf_op jit(solution)/shard_map/ppermute | solution.py:17
  113.2 3.0 %collective-permute-start = (f32[9,1,32,128]{3,2,1,0:T(8,128)S(1)}, f32[9,1,32,128]{3,2,1,0:T(8,128)S(1)}, u32[]{:S(2)}, u32[]{:S(2)}) collective-permute-start(f32[9,1,32,128]{3,2,1,0:T(8,128)S(1)} %get-tuple-element.218), channel_id=1, source_target_pairs={{0,1},{1,2},{2,3},{3,4},{4,5},{5,6},{6,7},{8,9},{9,10},{10,11},{11... | collective-permute-start | bytes 442376 | tf_op jit(solution)/shard_map/ppermute | solution.py:17
  116.2 1.9 collective-permute-start.1
  118.6 5.0 %collective-permute-done.1 = f32[9,1,32,128]{3,2,1,0:T(8,128)S(1)} collective-permute-done((f32[9,1,32,128]{3,2,1,0:T(8,128)S(1)}, f32[9,1,32,128]{3,2,1,0:T(8,128)S(1)}, u32[]{:S(2)}, u32[]{:S(2)}) %collective-permute-start.1) | collective-permute-done | bytes 147488 | tf_op jit(solution)/shard_map/ppermute | solution.py:17
  125.1 1.9 collective-permute-start.3
  127.0 2.4 %collective-permute-start.4 = (f32[9,1,32,128]{3,2,1,0:T(8,128)S(1)}, f32[9,1,32,128]{3,2,1,0:T(8,128)S(1)}, u32[]{:S(2)}, u32[]{:S(2)}) collective-permute-start(f32[9,1,32,128]{3,2,1,0:T(8,128)S(1)} %get-tuple-element.217), channel_id=1, source_target_pairs={{1,0},{2,1},{3,2},{4,3},{5,4},{6,5},{7,6},{9,8},{10,9},{11,10},{12... | collective-permute-start | bytes 442376 | tf_op jit(solution)/shard_map/ppermute | solution.py:17
  129.5 4.9 %collective-permute-done.4 = f32[9,1,32,128]{3,2,1,0:T(8,128)S(1)} collective-permute-done((f32[9,1,32,128]{3,2,1,0:T(8,128)S(1)}, f32[9,1,32,128]{3,2,1,0:T(8,128)S(1)}, u32[]{:S(2)}, u32[]{:S(2)}) %collective-permute-start.4) | collective-permute-done | bytes 147488 | tf_op jit(solution)/shard_map/ppermute | solution.py:17
  135.9 1.9 collective-permute-start.5
  137.9 2.4 %collective-permute-start.6 = (f32[9,1,32,128]{3,2,1,0:T(8,128)S(1)}, f32[9,1,32,128]{3,2,1,0:T(8,128)S(1)}, u32[]{:S(2)}, u32[]{:S(2)}) collective-permute-start(f32[9,1,32,128]{3,2,1,0:T(8,128)S(1)} %get-tuple-element.215), channel_id=1, source_target_pairs={{1,0},{2,1},{3,2},{4,3},{5,4},{6,5},{7,6},{9,8},{10,9},{11,10},{12... | collective-permute-start | bytes 442376 | tf_op jit(solution)/shard_map/ppermute | solution.py:17
  140.3 4.9 %collective-permute-done.6 = f32[9,1,32,128]{3,2,1,0:T(8,128)S(1)} collective-permute-done((f32[9,1,32,128]{3,2,1,0:T(8,128)S(1)}, f32[9,1,32,128]{3,2,1,0:T(8,128)S(1)}, u32[]{:S(2)}, u32[]{:S(2)}) %collective-permute-start.6) | collective-permute-done | bytes 147488 | tf_op jit(solution)/shard_map/ppermute | solution.py:17
  146.8 1.9 collective-permute-start.7
  148.7 2.4 %collective-permute-start.8 = (f32[9,1,32,128]{3,2,1,0:T(8,128)S(1)}, f32[9,1,32,128]{3,2,1,0:T(8,128)S(1)}, u32[]{:S(2)}, u32[]{:S(2)}) collective-permute-start(f32[9,1,32,128]{3,2,1,0:T(8,128)S(1)} %get-tuple-element.213), channel_id=1, source_target_pairs={{1,0},{2,1},{3,2},{4,3},{5,4},{6,5},{7,6},{9,8},{10,9},{11,10},{12... | collective-permute-start | bytes 442376 | tf_op jit(solution)/shard_map/ppermute | solution.py:17
  151.2 4.9 %collective-permute-done.8 = f32[9,1,32,128]{3,2,1,0:T(8,128)S(1)} collective-permute-done((f32[9,1,32,128]{3,2,1,0:T(8,128)S(1)}, f32[9,1,32,128]{3,2,1,0:T(8,128)S(1)}, u32[]{:S(2)}, u32[]{:S(2)}) %collective-permute-start.8) | collective-permute-done | bytes 147488 | tf_op jit(solution)/shard_map/ppermute | solution.py:17
  157.6 1.9 collective-permute-start.9
  159.5 2.4 %collective-permute-start.10 = (f32[9,1,32,128]{3,2,1,0:T(8,128)S(1)}, f32[9,1,32,128]{3,2,1,0:T(8,128)S(1)}, u32[]{:S(2)}, u32[]{:S(2)}) collective-permute-start(f32[9,1,32,128]{3,2,1,0:T(8,128)S(1)} %get-tuple-element.211), channel_id=1, source_target_pairs={{1,0},{2,1},{3,2},{4,3},{5,4},{6,5},{7,6},{9,8},{10,9},{11,10},{12... | collective-permute-start | bytes 442376 | tf_op jit(solution)/shard_map/ppermute | solution.py:17
  162.0 4.9 %collective-permute-done.10 = f32[9,1,32,128]{3,2,1,0:T(8,128)S(1)} collective-permute-done((f32[9,1,32,128]{3,2,1,0:T(8,128)S(1)}, f32[9,1,32,128]{3,2,1,0:T(8,128)S(1)}, u32[]{:S(2)}, u32[]{:S(2)}) %collective-permute-start.10) | collective-permute-done | bytes 147488 | tf_op jit(solution)/shard_map/ppermute | solution.py:17
  168.5 1.9 collective-permute-start.11
  170.4 2.4 %collective-permute-start.12 = (f32[9,1,32,128]{3,2,1,0:T(8,128)S(1)}, f32[9,1,32,128]{3,2,1,0:T(8,128)S(1)}, u32[]{:S(2)}, u32[]{:S(2)}) collective-permute-start(f32[9,1,32,128]{3,2,1,0:T(8,128)S(1)} %get-tuple-element.209), channel_id=1, source_target_pairs={{1,0},{2,1},{3,2},{4,3},{5,4},{6,5},{7,6},{9,8},{10,9},{11,10},{12... | collective-permute-start | bytes 442376 | tf_op jit(solution)/shard_map/ppermute | solution.py:17
  172.8 4.9 %collective-permute-done.12 = f32[9,1,32,128]{3,2,1,0:T(8,128)S(1)} collective-permute-done((f32[9,1,32,128]{3,2,1,0:T(8,128)S(1)}, f32[9,1,32,128]{3,2,1,0:T(8,128)S(1)}, u32[]{:S(2)}, u32[]{:S(2)}) %collective-permute-start.12) | collective-permute-done | bytes 147488 | tf_op jit(solution)/shard_map/ppermute | solution.py:17
  181.2 2.4 %collective-permute-start.14 = (f32[9,1,32,128]{3,2,1,0:T(8,128)S(1)}, f32[9,1,32,128]{3,2,1,0:T(8,128)S(1)}, u32[]{:S(2)}, u32[]{:S(2)}) collective-permute-start(f32[9,1,32,128]{3,2,1,0:T(8,128)S(1)} %get-tuple-element.207), channel_id=1, source_target_pairs={{1,0},{2,1},{3,2},{4,3},{5,4},{6,5},{7,6},{9,8},{10,9},{11,10},{12... | collective-permute-start | bytes 442376 | tf_op jit(solution)/shard_map/ppermute | solution.py:17
  183.7 4.9 %collective-permute-done.14 = f32[9,1,32,128]{3,2,1,0:T(8,128)S(1)} collective-permute-done((f32[9,1,32,128]{3,2,1,0:T(8,128)S(1)}, f32[9,1,32,128]{3,2,1,0:T(8,128)S(1)}, u32[]{:S(2)}, u32[]{:S(2)}) %collective-permute-start.14) | collective-permute-done | bytes 147488 | tf_op jit(solution)/shard_map/ppermute | solution.py:17
  190.1 1.9 collective-permute-start.15
  192.1 2.4 %collective-permute-start.16 = (f32[9,1,32,128]{3,2,1,0:T(8,128)S(1)}, f32[9,1,32,128]{3,2,1,0:T(8,128)S(1)}, u32[]{:S(2)}, u32[]{:S(2)}) collective-permute-start(f32[9,1,32,128]{3,2,1,0:T(8,128)S(1)} %get-tuple-element.205), channel_id=1, source_target_pairs={{1,0},{2,1},{3,2},{4,3},{5,4},{6,5},{7,6},{9,8},{10,9},{11,10},{12... | collective-permute-start | bytes 442376 | tf_op jit(solution)/shard_map/ppermute | solution.py:17
  194.5 4.9 %collective-permute-done.16 = f32[9,1,32,128]{3,2,1,0:T(8,128)S(1)} collective-permute-done((f32[9,1,32,128]{3,2,1,0:T(8,128)S(1)}, f32[9,1,32,128]{3,2,1,0:T(8,128)S(1)}, u32[]{:S(2)}, u32[]{:S(2)}) %collective-permute-start.16) | collective-permute-done | bytes 147488 | tf_op jit(solution)/shard_map/ppermute | solution.py:17
  (252 shorter events, 22.4 us)
Async XLA Ops:
  0.6 3.2 %copy-start = (f32[16,3]{0,1:T(4,128)S(1)}, f32[16,3]{0,1:T(4,128)}, u32[]{:S(2)}) copy-start(f32[16,3]{0,1:T(4,128)} %param.18) | copy-start | bytes 580
  0.6 6.0 %copy-start.1 = (f32[8,6,4,8]{3,2,1,0:T(4,128)S(1)}, f32[8,6,4,8]{3,2,1,0:T(4,128)}, u32[]{:S(2)}) copy-start(f32[8,6,4,8]{3,2,1,0:T(4,128)} %param.16) | copy-start | bytes 18436
  6.6 0.7 copy-start.7
  93.7 0.8 copy-start.4
  94.4 0.8 copy-start.5
  94.4 0.8 copy-start.6
  95.2 17.9 %copy-start.3 = (f32[3,4,32,128]{3,2,1,0:T(8,128)S(1)}, f32[3,4,32,128]{3,2,1,0:T(8,128)}, u32[]{:S(2)}) copy-start(f32[3,4,32,128]{3,2,1,0:T(8,128)} %param.11) | copy-start | bytes 589828
  95.2 17.9 %copy-start.2 = (f32[6,4,32,128]{3,2,1,0:T(8,128)S(1)}, f32[6,4,32,128]{3,2,1,0:T(8,128)}, u32[]{:S(2)}) copy-start(f32[6,4,32,128]{3,2,1,0:T(8,128)} %param.12) | copy-start | bytes 1179652
  95.3 22.9 %collective-permute-start.2 = (f32[13824]{0:T(1024)S(1)}, f32[13824]{0:T(1024)S(1)}, u32[]{:S(2)}, u32[]{:S(2)}) collective-permute-start(f32[13824]{0:T(1024)S(1)} %pad_maximum_fusion.39), channel_id=1, source_target_pairs={{1,0},{2,1},{3,2},{4,3},{5,4},{6,5},{7,6},{9,8},{10,9},{11,10},{12... | collective-permute-start | bytes 165896 | tf_op jit(solution)/shard_map/ppermute | solution.py:17
  113.2 5.3 %collective-permute-start = (f32[9,1,32,128]{3,2,1,0:T(8,128)S(1)}, f32[9,1,32,128]{3,2,1,0:T(8,128)S(1)}, u32[]{:S(2)}, u32[]{:S(2)}) collective-permute-start(f32[9,1,32,128]{3,2,1,0:T(8,128)S(1)} %get-tuple-element.218), channel_id=1, source_target_pairs={{0,1},{1,2},{2,3},{3,4},{4,5},{5,6},{6,7},{8,9},{9,10},{10,11},{11... | collective-permute-start | bytes 442376 | tf_op jit(solution)/shard_map/ppermute | solution.py:17
  116.2 7.4 %collective-permute-start.1 = (f32[9,1,32,128]{3,2,1,0:T(8,128)S(1)}, f32[9,1,32,128]{3,2,1,0:T(8,128)S(1)}, u32[]{:S(2)}, u32[]{:S(2)}) collective-permute-start(f32[9,1,32,128]{3,2,1,0:T(8,128)S(1)} %get-tuple-element.219), channel_id=1, source_target_pairs={{1,0},{2,1},{3,2},{4,3},{5,4},{6,5},{7,6},{9,8},{10,9},{11,10},{12... | collective-permute-start | bytes 442376 | tf_op jit(solution)/shard_map/ppermute | solution.py:17
  125.1 4.4 %collective-permute-start.3 = (f32[9,1,32,128]{3,2,1,0:T(8,128)S(1)}, f32[9,1,32,128]{3,2,1,0:T(8,128)S(1)}, u32[]{:S(2)}, u32[]{:S(2)}) collective-permute-start(f32[9,1,32,128]{3,2,1,0:T(8,128)S(1)} %get-tuple-element.216), channel_id=1, source_target_pairs={{0,1},{1,2},{2,3},{3,4},{4,5},{5,6},{6,7},{8,9},{9,10},{10,11},{11... | collective-permute-start | bytes 442376 | tf_op jit(solution)/shard_map/ppermute | solution.py:17
  127.0 7.4 %collective-permute-start.4 = (f32[9,1,32,128]{3,2,1,0:T(8,128)S(1)}, f32[9,1,32,128]{3,2,1,0:T(8,128)S(1)}, u32[]{:S(2)}, u32[]{:S(2)}) collective-permute-start(f32[9,1,32,128]{3,2,1,0:T(8,128)S(1)} %get-tuple-element.217), channel_id=1, source_target_pairs={{1,0},{2,1},{3,2},{4,3},{5,4},{6,5},{7,6},{9,8},{10,9},{11,10},{12... | collective-permute-start | bytes 442376 | tf_op jit(solution)/shard_map/ppermute | solution.py:17
  135.9 4.3 %collective-permute-start.5 = (f32[9,1,32,128]{3,2,1,0:T(8,128)S(1)}, f32[9,1,32,128]{3,2,1,0:T(8,128)S(1)}, u32[]{:S(2)}, u32[]{:S(2)}) collective-permute-start(f32[9,1,32,128]{3,2,1,0:T(8,128)S(1)} %get-tuple-element.214), channel_id=1, source_target_pairs={{0,1},{1,2},{2,3},{3,4},{4,5},{5,6},{6,7},{8,9},{9,10},{10,11},{11... | collective-permute-start | bytes 442376 | tf_op jit(solution)/shard_map/ppermute | solution.py:17
  137.9 7.4 %collective-permute-start.6 = (f32[9,1,32,128]{3,2,1,0:T(8,128)S(1)}, f32[9,1,32,128]{3,2,1,0:T(8,128)S(1)}, u32[]{:S(2)}, u32[]{:S(2)}) collective-permute-start(f32[9,1,32,128]{3,2,1,0:T(8,128)S(1)} %get-tuple-element.215), channel_id=1, source_target_pairs={{1,0},{2,1},{3,2},{4,3},{5,4},{6,5},{7,6},{9,8},{10,9},{11,10},{12... | collective-permute-start | bytes 442376 | tf_op jit(solution)/shard_map/ppermute | solution.py:17
  146.8 4.3 %collective-permute-start.7 = (f32[9,1,32,128]{3,2,1,0:T(8,128)S(1)}, f32[9,1,32,128]{3,2,1,0:T(8,128)S(1)}, u32[]{:S(2)}, u32[]{:S(2)}) collective-permute-start(f32[9,1,32,128]{3,2,1,0:T(8,128)S(1)} %get-tuple-element.212), channel_id=1, source_target_pairs={{0,1},{1,2},{2,3},{3,4},{4,5},{5,6},{6,7},{8,9},{9,10},{10,11},{11... | collective-permute-start | bytes 442376 | tf_op jit(solution)/shard_map/ppermute | solution.py:17
  148.7 7.4 %collective-permute-start.8 = (f32[9,1,32,128]{3,2,1,0:T(8,128)S(1)}, f32[9,1,32,128]{3,2,1,0:T(8,128)S(1)}, u32[]{:S(2)}, u32[]{:S(2)}) collective-permute-start(f32[9,1,32,128]{3,2,1,0:T(8,128)S(1)} %get-tuple-element.213), channel_id=1, source_target_pairs={{1,0},{2,1},{3,2},{4,3},{5,4},{6,5},{7,6},{9,8},{10,9},{11,10},{12... | collective-permute-start | bytes 442376 | tf_op jit(solution)/shard_map/ppermute | solution.py:17
  157.6 4.4 %collective-permute-start.9 = (f32[9,1,32,128]{3,2,1,0:T(8,128)S(1)}, f32[9,1,32,128]{3,2,1,0:T(8,128)S(1)}, u32[]{:S(2)}, u32[]{:S(2)}) collective-permute-start(f32[9,1,32,128]{3,2,1,0:T(8,128)S(1)} %get-tuple-element.210), channel_id=1, source_target_pairs={{0,1},{1,2},{2,3},{3,4},{4,5},{5,6},{6,7},{8,9},{9,10},{10,11},{11... | collective-permute-start | bytes 442376 | tf_op jit(solution)/shard_map/ppermute | solution.py:17
  159.5 7.4 %collective-permute-start.10 = (f32[9,1,32,128]{3,2,1,0:T(8,128)S(1)}, f32[9,1,32,128]{3,2,1,0:T(8,128)S(1)}, u32[]{:S(2)}, u32[]{:S(2)}) collective-permute-start(f32[9,1,32,128]{3,2,1,0:T(8,128)S(1)} %get-tuple-element.211), channel_id=1, source_target_pairs={{1,0},{2,1},{3,2},{4,3},{5,4},{6,5},{7,6},{9,8},{10,9},{11,10},{12... | collective-permute-start | bytes 442376 | tf_op jit(solution)/shard_map/ppermute | solution.py:17
  168.5 4.3 %collective-permute-start.11 = (f32[9,1,32,128]{3,2,1,0:T(8,128)S(1)}, f32[9,1,32,128]{3,2,1,0:T(8,128)S(1)}, u32[]{:S(2)}, u32[]{:S(2)}) collective-permute-start(f32[9,1,32,128]{3,2,1,0:T(8,128)S(1)} %get-tuple-element.208), channel_id=1, source_target_pairs={{0,1},{1,2},{2,3},{3,4},{4,5},{5,6},{6,7},{8,9},{9,10},{10,11},{11... | collective-permute-start | bytes 442376 | tf_op jit(solution)/shard_map/ppermute | solution.py:17
  170.4 7.4 %collective-permute-start.12 = (f32[9,1,32,128]{3,2,1,0:T(8,128)S(1)}, f32[9,1,32,128]{3,2,1,0:T(8,128)S(1)}, u32[]{:S(2)}, u32[]{:S(2)}) collective-permute-start(f32[9,1,32,128]{3,2,1,0:T(8,128)S(1)} %get-tuple-element.209), channel_id=1, source_target_pairs={{1,0},{2,1},{3,2},{4,3},{5,4},{6,5},{7,6},{9,8},{10,9},{11,10},{12... | collective-permute-start | bytes 442376 | tf_op jit(solution)/shard_map/ppermute | solution.py:17
  179.3 4.3 %collective-permute-start.13 = (f32[9,1,32,128]{3,2,1,0:T(8,128)S(1)}, f32[9,1,32,128]{3,2,1,0:T(8,128)S(1)}, u32[]{:S(2)}, u32[]{:S(2)}) collective-permute-start(f32[9,1,32,128]{3,2,1,0:T(8,128)S(1)} %get-tuple-element.206), channel_id=1, source_target_pairs={{0,1},{1,2},{2,3},{3,4},{4,5},{5,6},{6,7},{8,9},{9,10},{10,11},{11... | collective-permute-start | bytes 442376 | tf_op jit(solution)/shard_map/ppermute | solution.py:17
  181.2 7.4 %collective-permute-start.14 = (f32[9,1,32,128]{3,2,1,0:T(8,128)S(1)}, f32[9,1,32,128]{3,2,1,0:T(8,128)S(1)}, u32[]{:S(2)}, u32[]{:S(2)}) collective-permute-start(f32[9,1,32,128]{3,2,1,0:T(8,128)S(1)} %get-tuple-element.207), channel_id=1, source_target_pairs={{1,0},{2,1},{3,2},{4,3},{5,4},{6,5},{7,6},{9,8},{10,9},{11,10},{12... | collective-permute-start | bytes 442376 | tf_op jit(solution)/shard_map/ppermute | solution.py:17
  190.1 4.3 %collective-permute-start.15 = (f32[9,1,32,128]{3,2,1,0:T(8,128)S(1)}, f32[9,1,32,128]{3,2,1,0:T(8,128)S(1)}, u32[]{:S(2)}, u32[]{:S(2)}) collective-permute-start(f32[9,1,32,128]{3,2,1,0:T(8,128)S(1)} %get-tuple-element.204), channel_id=1, source_target_pairs={{0,1},{1,2},{2,3},{3,4},{4,5},{5,6},{6,7},{8,9},{9,10},{10,11},{11... | collective-permute-start | bytes 442376 | tf_op jit(solution)/shard_map/ppermute | solution.py:17
  192.1 7.4 %collective-permute-start.16 = (f32[9,1,32,128]{3,2,1,0:T(8,128)S(1)}, f32[9,1,32,128]{3,2,1,0:T(8,128)S(1)}, u32[]{:S(2)}, u32[]{:S(2)}) collective-permute-start(f32[9,1,32,128]{3,2,1,0:T(8,128)S(1)} %get-tuple-element.205), channel_id=1, source_target_pairs={{1,0},{2,1},{3,2},{4,3},{5,4},{6,5},{7,6},{9,8},{10,9},{11,10},{12... | collective-permute-start | bytes 442376 | tf_op jit(solution)/shard_map/ppermute | solution.py:17
where the time goes:
time: 203 us; the launch traced here: 202 us
  blocking collectives  58.7 us (29%)
  starting transfers between devices  53 us (26%)
  waiting for transfers between devices  39.4 us (19%)
  local copies, waits for them, and re-layouts  33.4 us (16%)
  other arithmetic  8.73 us (4%)
  between operations  6.28 us (3%)
  loops' own time  2.77 us (1%)
    psum x4, blocking collectives, from_root(): return lax.psum(jnp.where(mine, array, jnp.zeros_like(array)), axis)  58.7 us
    ppermute x17, starting transfers between devices, from_behind(): lax.ppermute(value, axis, [(source, source + steps) for source in range(f...  53 us
    ppermute x17, waiting for transfers between devices, from_behind(): lax.ppermute(value, axis, [(source, source + steps) for source in range(f...  39.4 us
    dynamic_update_slice x4, local copies, waits for them, and re-layouts, place(): return lax.dynamic_update_slice_in_dim(plane, piece, index * columns, 3)  22.4 us
  transfers between devices with their start and end apart: 17, of which 8 were waited for; matrix products, arithmetic and copies ran while one was open for 0% of the time, Pallas kernels for 0%

commit v1 on v0

v1 whole, which is shorter than its diff:
```python
import functools

import jax
import jax.numpy as jnp
from jax import lax
from jax.experimental import pallas as pl
from jax.experimental.pallas import tpu as pltpu
from jax.sharding import PartitionSpec as P

DT = 0.15
MESH = pl.DeviceIdType.MESH
ABOVE = 1
BELOW = 1
TOP = 8
CHUNK = 32
CROSS = (0, 3, 4)


def kernel(
    groups,
    slabs,
    steps,
    owner_ref,
    table_ref,
    order_ref,
    vel_ref,
    sig_ref,
    lam_ref,
    mu_ref,
    buoy_ref,
    block_ref,
    vel_out,
    sig_out,
    V,
    S,
    M,
    E,
    raw,
    blocks,
    rows,
    per_step,
    down_in,
    up_in,
    down_out,
    up_out,
    vel_last,
    sig_last,
    local_sem,
    block_send,
    block_recv,
    ghost_send,
    ghost_recv,
    down_send,
    down_recv,
    up_send,
    up_recv,
    out_sem,
):
    planes, width, depth = vel_ref.shape[1:]
    n = BELOW + planes + ABOVE
    own = BELOW
    group = lax.axis_index("cand")
    slab = lax.axis_index("slab")
    has_lower = slab > 0
    has_upper = slab < slabs - 1
    lower, upper = slab - 1, slab + 1
    dplane = own + ABOVE
    uplane = own + planes - 1 - BELOW

    barrier = pltpu.get_barrier_semaphore()
    for k in range(1, groups):
        pl.semaphore_signal(
            barrier, inc=1, device_id=(lax.rem(group + k, groups), slab), device_id_type=MESH
        )

    @pl.when(has_lower)
    def _():
        for k in range(groups):
            pl.semaphore_signal(
                barrier, inc=1, device_id=(lax.rem(group + k, groups), lower), device_id_type=MESH
            )

    @pl.when(has_upper)
    def _():
        for k in range(groups):
            pl.semaphore_signal(
                barrier, inc=1, device_id=(lax.rem(group + k, groups), upper), device_id_type=MESH
            )

    loads = [
        pltpu.make_async_copy(lam_ref, raw.at[0], local_sem.at[0]),
        pltpu.make_async_copy(mu_ref, raw.at[1], local_sem.at[1]),
        pltpu.make_async_copy(buoy_ref, raw.at[2], local_sem.at[2]),
        pltpu.make_async_copy(block_ref, blocks.at[1, group], local_sem.at[3]),
        pltpu.make_async_copy(
            vel_ref, V.at[:, pl.ds(own, planes), pl.ds(0, width)], local_sem.at[4]
        ),
        pltpu.make_async_copy(
            sig_ref, S.at[:, pl.ds(own, planes), pl.ds(TOP, width)], local_sem.at[5]
        ),
    ]
    for load in loads:
        load.start()

    V[:, :, width:] = jnp.zeros((3, n, V.shape[2] - width, depth), jnp.float32)
    S[:, :, :TOP] = jnp.zeros((6, n, TOP, depth), jnp.float32)

    @pl.when(jnp.logical_not(has_lower))
    def _():
        up_in[...] = jnp.zeros_like(up_in)
        blocks[0] = jnp.zeros(blocks.shape[1:], jnp.float32)
        if BELOW:
            V[:, :BELOW, :width] = jnp.zeros((3, BELOW, width, depth), jnp.float32)
            S[:, :BELOW, TOP:] = jnp.zeros((6, BELOW, width, depth), jnp.float32)
            M[:, :BELOW] = jnp.zeros((3, BELOW, width, depth), jnp.float32)

    @pl.when(jnp.logical_not(has_upper))
    def _():
        down_in[...] = jnp.zeros_like(down_in)
        blocks[2] = jnp.zeros(blocks.shape[1:], jnp.float32)
        if ABOVE:
            V[:, n - ABOVE :, :width] = jnp.zeros((3, ABOVE, width, depth), jnp.float32)
            S[:, n - ABOVE :, TOP:] = jnp.zeros((6, ABOVE, width, depth), jnp.float32)
            M[:, n - ABOVE :] = jnp.zeros((3, ABOVE, width, depth), jnp.float32)

    lane = lax.broadcasted_iota(jnp.int32, (width, depth), 1)
    zone = lax.broadcasted_iota(jnp.int32, (planes, width, depth), 2) >= depth // 2
    chosen = order_ref[group]
    for load in loads[:3]:
        load.wait()
    for which in range(3):
        scale = jnp.where(zone, table_ref[chosen, which] * DT, DT)
        M[which, own : own + planes] = raw[which].astype(jnp.float32) * scale

    sides = has_lower.astype(jnp.int32) + has_upper.astype(jnp.int32)
    pl.semaphore_wait(barrier, groups - 1 + groups * sides)

    def block_copy(level, slot, to, index):
        return pltpu.make_async_remote_copy(
            src_ref=block_ref,
            dst_ref=blocks.at[level, slot],
            send_sem=block_send.at[level, index],
            recv_sem=block_recv.at[level, slot],
            device_id=to,
            device_id_type=MESH,
        )

    def ghost_copies(down):
        count, to = (ABOVE, lower) if down else (BELOW, upper)
        base = 0 if down else 3
        source = 0 if down else planes - BELOW
        target = own + planes if down else 0
        pairs = []
        if count:
            there = pl.ds(target, count)
            pairs = [
                (sig_ref.at[:, pl.ds(source, count)], S.at[:, there, pl.ds(TOP, width)]),
                (vel_ref.at[:, pl.ds(source, count)], V.at[:, there, pl.ds(0, width)]),
                (M.at[:, pl.ds(own + source, count)], M.at[:, there]),
            ]
        else:
            base = 3
        if not down:
            edge = planes - 1 - BELOW
            pairs.append((sig_ref.at[0, edge], up_in.at[0, 0]))
            pairs.append((sig_ref.at[pl.ds(3, 2), edge], up_in.at[0, pl.ds(1, 2)]))
        return [
            pltpu.make_async_remote_copy(
                src_ref=src,
                dst_ref=dst,
                send_sem=ghost_send.at[base + at],
                recv_sem=ghost_recv.at[base + at],
                device_id=(group, to),
                device_id_type=MESH,
            )
            for at, (src, dst) in enumerate(pairs)
        ]

    def level_slots(level):
        return range(1 if level == 1 else 0, groups)

    def send_blocks(level, to):
        for k in level_slots(level):
            block_copy(level, group, (lax.rem(group + k, groups), to), k).start()

    def each_side(low, high):
        pl.when(has_lower)(low)
        pl.when(has_upper)(high)

    send_blocks(1, slab)

    def first_low():
        send_blocks(2, lower)
        for copy in ghost_copies(True):
            copy.start()

    def first_high():
        send_blocks(0, upper)
        for copy in ghost_copies(False):
            copy.start()

    each_side(first_low, first_high)

    def take_blocks(level, to):
        for k in level_slots(level):
            slot = lax.rem(group + k, groups)
            block_copy(level, slot, (slot, to), k).wait_recv()

    loads[3].wait()
    take_blocks(1, slab)
    each_side(lambda: take_blocks(0, lower), lambda: take_blocks(2, upper))
    columns = width // groups
    for level in range(3):
        for j in range(groups):
            rows[level, j * columns : (j + 1) * columns] = blocks[level, owner_ref[j]]
    halves = 128 // CHUNK
    for t in range(steps):
        at = 128 * (t // halves)
        for level in range(3):
            piece = rows[level, :, at : at + 128]
            shift = (t % halves) * CHUNK
            per_step[t, level] = pltpu.roll(piece, 128 - shift, 1) if shift else piece

    source_level = depth // 8

    def spread(t, carry):
        for i in range(n):
            x = i - own
            level = 0 if x < 0 else 2 if x >= planes else 1
            value = per_step[t, level]
            for c in range(6):
                at = c * planes + x % planes
                moved = pltpu.roll(value, (source_level - at) % depth, 1)
                E[t, c, i] = jnp.where(lane == source_level, moved, 0.0)
        return carry

    lax.fori_loop(0, steps, spread, 0)

    for load in loads[4:]:
        load.wait()

    def ghosts_here():
        for copy in ghost_copies(True):
            copy.wait_recv()

    def ghosts_below_here():
        for copy in ghost_copies(False):
            copy.wait_recv()

    each_side(ghosts_below_here, ghosts_here)

    def before(f):
        return jnp.where(lane == 0, 0.0, pltpu.roll(f, 1, 1))

    def after(f):
        return jnp.where(lane == depth - 1, 0.0, pltpu.roll(f, depth - 1, 1))

    def here(c, i):
        return S[c, i, TOP : TOP + width]

    def south(c, i):
        return S[c, i, TOP - 1 : TOP - 1 + width]

    def new_vel(i, t):
        if i == 0:
            west = [up_in[t, c] for c in range(3)]
        else:
            west = [here(c, i - 1) for c in CROSS]
        sxx, syy, szz, sxy, sxz, syz = (here(c, i) for c in range(6))
        b = M[2, i]
        ax = (sxx - west[0]) + (sxy - south(3, i)) + (sxz - before(sxz)) + E[t, 0, i]
        ay = (sxy - west[1]) + (syy - south(1, i)) + (syz - before(syz)) + E[t, 1, i]
        az = (sxz - west[2]) + (syz - south(5, i)) + (szz - before(szz)) + E[t, 2, i]
        return [V[c, i, :width] + b * a for c, a in enumerate((ax, ay, az))]

    def new_sig(i, t):
        vx, vy, vz = (V[c, i, :width] for c in range(3))
        nx, ny, nz = (V[c, i, 1 : 1 + width] for c in range(3))
        if i == n - 1:
            ex, ey, ez = (down_in[t, c] for c in range(3))
        else:
            ex, ey, ez = (V[c, i + 1, :width] for c in range(3))
        lam, mu = M[0, i], M[1, i]
        mu2 = mu + mu
        xx, yy, zz = ex - vx, ny - vy, after(vz) - vz
        zz_in = E[t, 5, i]
        spread_all = lam * (xx + yy + zz)
        return [
            here(0, i) + (spread_all + mu2 * xx),
            here(1, i) + (spread_all + mu2 * yy),
            here(2, i) + (spread_all + mu2 * zz + (lam + mu2) * zz_in),
            here(3, i) + mu * ((nx - vx) + (ey - vy)),
            here(4, i) + mu * ((after(vx) - vx) + (ez - vz) + E[t, 3, i]),
            here(5, i) + mu * ((after(vy) - vy) + (nz - vz) + E[t, 4, i]),
        ]

    def set_vel(i, t):
        values = new_vel(i, t)
        for c in range(3):
            V[c, i, :width] = values[c]
        return values

    def set_sig(i, t):
        values = new_sig(i, t)
        for c in range(6):
            S[c, i, TOP : TOP + width] = values[c]
        return values

    def down_copy(t):
        return pltpu.make_async_remote_copy(
            src_ref=down_out.at[t],
            dst_ref=down_in.at[t],
            send_sem=down_send.at[t],
            recv_sem=down_recv.at[t],
            device_id=(group, lower),
            device_id_type=MESH,
        )

    def up_copy(t):
        return pltpu.make_async_remote_copy(
            src_ref=up_out.at[t],
            dst_ref=up_in.at[t + 1],
            send_sem=up_send.at[t],
            recv_sem=up_recv.at[t],
            device_id=(group, upper),
            device_id_type=MESH,
        )

    last_up = steps - 2 - BELOW

    def finish_top(t):
        @pl.when(has_upper)
        def _():
            down_copy(t - 1).wait_recv()

        set_sig(n - 1, t - 1)

    def send_up(t):
        values = set_sig(uplane, t)

        @pl.when(jnp.logical_and(has_upper, t <= last_up))
        def _():
            for at, c in enumerate(CROSS):
                up_out[t, at] = values[c]
            up_copy(t).start()

    def one_step(t, carry):
        values = set_vel(dplane, t)

        @pl.when(has_lower)
        def _():
            for c in range(3):
                down_out[t, c] = values[c]
            down_copy(t).start()

        done = [dplane]
        early = uplane + 1 <= n - 2
        if early:
            for i in (uplane, uplane + 1):
                if i not in done and i > 0:
                    set_vel(i, t)
                    done.append(i)
            send_up(t)
        for i in range(1, n - 1):
            if i not in done:
                set_vel(i, t)

        @pl.when(t > 0)
        def _():
            finish_top(t)

        set_vel(n - 1, t)
        if not early:
            send_up(t)
        for i in range(n - 2, 0, -1):
            if i != uplane:
                set_sig(i, t)

        @pl.when(jnp.logical_and(has_lower, t > 0))
        def _():
            up_copy(t - 1).wait_recv()

        set_vel(0, t)
        set_sig(0, t)
        return carry

    lax.fori_loop(0, steps - 1, one_step, 0)

    t = steps - 1
    out_copies = []

    def store(ref, out, i, values, sem):
        x = i - own
        for c, value in enumerate(values):
            ref[c, x] = value
        copy = pltpu.make_async_copy(ref.at[:, x], out.at[0, :, x], out_sem.at[sem, x])
        copy.start()
        out_copies.append(copy)

    if BELOW == 0:

        @pl.when(has_lower)
        def _():
            up_copy(t - 1).wait_recv()

    for i in range(own, own + planes):
        values = set_vel(i, t)
        store(vel_last, vel_out, i, values, 0)
    for i in range(own, own + planes - 1):
        store(sig_last, sig_out, i, new_sig(i, t), 1)
    finish_top(t)
    set_vel(own + planes, t)
    i = own + planes - 1
    store(sig_last, sig_out, i, new_sig(i, t), 1)

    for k in level_slots(1):
        block_copy(1, group, (lax.rem(group + k, groups), slab), k).wait_send()

    def sent_low():
        for k in level_slots(2):
            block_copy(2, group, (lax.rem(group + k, groups), lower), k).wait_send()
        for copy in ghost_copies(True):
            copy.wait_send()
        for s in range(steps - 1):
            down_copy(s).wait_send()

    def sent_high():
        for k in level_slots(0):
            block_copy(0, group, (lax.rem(group + k, groups), upper), k).wait_send()
        for copy in ghost_copies(False):
            copy.wait_send()
        for s in range(last_up + 1):
            up_copy(s).wait_send()

    each_side(sent_low, sent_high)
    for copy in out_copies:
        copy.wait()


def body(
    groups,
    slabs,
    velocity,
    stress,
    lame_lambda,
    shear_modulus,
    buoyancy,
    surface,
    block_owner,
    candidates,
    candidate_of_group,
):
    planes, width, depth = velocity.shape[1:]
    steps, parts = surface.shape[:2]
    columns = surface.shape[3]
    n = BELOW + planes + ABOVE
    packed = surface.transpose(3, 0, 1, 2).reshape(columns, steps, parts * planes)
    packed = jnp.pad(packed, ((0, 0), (0, 0), (0, CHUNK - parts * planes)))
    packed = packed.reshape(columns, steps * CHUNK)
    lanes = steps * CHUNK
    any_space = pl.BlockSpec(memory_space=pl.ANY)
    scalars = pl.BlockSpec(memory_space=pltpu.SMEM)
    f32 = jnp.float32
    message = pltpu.VMEM((steps, 3, width, depth), f32)
    dma = pltpu.SemaphoreType.DMA
    return pl.pallas_call(
        functools.partial(kernel, groups, slabs, steps),
        out_shape=(
            jax.ShapeDtypeStruct((1, 3, planes, width, depth), f32),
            jax.ShapeDtypeStruct((1, 6, planes, width, depth), f32),
        ),
        in_specs=[scalars] * 3 + [any_space] * 6,
        out_specs=(any_space, any_space),
        scratch_shapes=[
            pltpu.VMEM((3, n, width + 8, depth), f32),
            pltpu.VMEM((6, n, width + TOP, depth), f32),
            pltpu.VMEM((3, n, width, depth), f32),
            pltpu.VMEM((steps, 6, n, width, depth), f32),
            pltpu.VMEM((3, planes, width, depth), jnp.bfloat16),
            pltpu.VMEM((3, groups, columns, lanes), f32),
            pltpu.VMEM((3, width, lanes), f32),
            pltpu.VMEM((steps, 3, width, 128), f32),
            message,
            message,
            message,
            message,
            pltpu.VMEM((3, planes, width, depth), f32),
            pltpu.VMEM((6, planes, width, depth), f32),
            dma((6,)),
            dma((3, groups)),
            dma((3, groups)),
            dma((8,)),
            dma((8,)),
            dma((steps,)),
            dma((steps,)),
            dma((steps,)),
            dma((steps,)),
            dma((2, planes)),
        ],
        compiler_params=pltpu.CompilerParams(
            collective_id=0, has_side_effects=True, vmem_limit_bytes=40 * 1024 * 1024
        ),
    )(
        block_owner,
        candidates,
        candidate_of_group,
        velocity,
        stress,
        lame_lambda,
        shear_modulus,
        buoyancy,
        packed,
    )


def solution(mesh):
    in_specs = (
        P(None, "slab", None, None),
        P(None, "slab", None, None),
        P("slab", None, None),
        P("slab", None, None),
        P("slab", None, None),
        P(None, None, "slab", "cand"),
        P(),
        P(),
        P(),
    )
    out_specs = (P("cand", None, "slab", None, None), P("cand", None, "slab", None, None))
    return jax.shard_map(
        functools.partial(body, mesh.shape["cand"], mesh.shape["slab"]),
        mesh=mesh,
        in_specs=in_specs,
        out_specs=out_specs,
        check_vma=False,
    )
```

time: 203 us -> 35.2 us (0.17)
  blocking collectives: 58.7 us -> 0 us
  starting transfers between devices: 53 us -> 0 us
  waiting for transfers between devices: 39.4 us -> 0 us
  Pallas kernels: 0 us -> 27.7 us
  local copies, waits for them, and re-layouts: 33.4 us -> 6.46 us
  other arithmetic: 8.73 us -> 0 us
  between operations: 6.28 us -> 0.68 us
  loops' own time: 2.77 us -> 0 us
    psum x4 -> x0, blocking collectives: 58.7 us -> none  [from_root(): return lax.psum(jnp.where(mine, array, jnp.zeros_like(array)), axis)]
    ppermute x17 -> x0, starting transfers between devices: 53 us -> none  [from_behind(): lax.ppermute(value, axis, [(source, source + steps) for source in range(f...]
    ppermute x17 -> x0, waiting for transfers between devices: 39.4 us -> none  [from_behind(): lax.ppermute(value, axis, [(source, source + steps) for source in range(f...]
    pallas_call x0 -> x1, Pallas kernels: none -> 27.7 us  [body(): pl.pallas_call(functools.partial(kernel, groups, slabs, steps), out_shape...]
    dynamic_update_slice x4 -> x0, local copies, waits for them, and re-layouts: 22.4 us -> none  [place(): return lax.dynamic_update_slice_in_dim(plane, piece, index * columns, 3)]
    another operation x34 -> x0, other arithmetic: 3.77 us -> none  [the longest x23 2.94 us: advance_velocity(): return vel + DT * buoy * jnp.stack([acc_x, acc_y, acc_z])]
    dynamic_slice x6 -> x0, local copies, waits for them, and re-layouts: 3.7 us -> none  [the longest x4 2.35 us: place(): piece = from_root(surface, 'cand', block_owner[index])]
    slice x75 -> x0, local copies, waits for them, and re-layouts: 3.4 us -> none  [the longest x24 2 us: plus_z(): return jnp.concatenate([field[..., 1:], edge], axis=-1) - field]
  transfers between devices with their start and end apart: 17 -> 0, of which waited for: 8 -> 0; matrix products, arithmetic and copies ran while one was open for 0% -> 0% of each run, Pallas kernels for 0% -> 0%
where the time goes in v1:
time: 35.2 us; the launch traced here: 34.8 us
  Pallas kernels  27.7 us (79%)
  local copies, waits for them, and re-layouts  6.46 us (18%)
  between operations  0.68 us (2%)
    pallas_call x1, Pallas kernels, body(): pl.pallas_call(functools.partial(kernel, groups, slabs, steps), out_shape...  27.7 us
    unnamed x17, local copies, waits for them, and re-layouts  5.4 us
    reshape x1, local copies, waits for them, and re-layouts, body(): surface.transpose(3, 0, 1, 2).reshape(columns, steps, parts * planes)  0.97 us

profile of v1, /device:TPU:3, one launch (start us, length us, event | category | flops | bytes accessed | tf_op | source)
XLA Modules:
  0.0 34.8 jit_solution(13364336062819507068)
XLA Ops:
  0.6 0.0 copy-start.1
  0.6 0.8 %copy.12.table_ref = f32[16,3]{1,0:T(8,128)S(1)} copy(f32[16,3]{0,1:T(4,128)} %param.16) | data formatting | bytes 384 | tf_op args[7]
  1.4 1.0 %copy.11 = f32[8,8,24]{2,1,0:T(8,128)S(1)} copy(f32[8,8,24]{0,2,1:T(8,128)} %bitcast.3) | data formatting | bytes 12288 | tf_op jit(solution)/shard_map/reshape | solution.py:457
  2.4 0.0 copy-start.2
  2.4 0.0 copy-start.5
  2.5 0.0 copy-start.6
  2.5 0.1 reshape.11.block_ref
  2.5 0.0 copy-done.1
  2.5 0.6 %copy-done.2 = bf16[4,32,128]{2,1,0:T(8,128)(2,1)S(1)} copy-done((bf16[4,32,128]{2,1,0:T(8,128)(2,1)S(1)}, bf16[4,32,128]{2,1,0:T(8,128)(2,1)}, u32[]{:S(2)}) %copy-start.2) | copy-done | bytes 32792
  3.2 0.0 copy-done.5
  3.2 0.0 copy-done.6
  3.2 0.0 copy-start
  3.2 1.0 %copy-done = f32[6,4,32,128]{3,2,1,0:T(8,128)S(1)} copy-done((f32[6,4,32,128]{3,2,1,0:T(8,128)S(1)}, f32[6,4,32,128]{3,2,1,0:T(8,128)}, u32[]{:S(2)}) %copy-start) | copy-done | bytes 393240
  4.2 0.0 copy-start.3
  4.2 0.8 %copy-done.3 = bf16[4,32,128]{2,1,0:T(8,128)(2,1)S(1)} copy-done((bf16[4,32,128]{2,1,0:T(8,128)(2,1)S(1)}, bf16[4,32,128]{2,1,0:T(8,128)(2,1)}, u32[]{:S(2)}) %copy-start.3) | copy-done | bytes 32792
  5.0 0.0 copy-start.4
  5.0 0.8 %copy-done.4 = bf16[4,32,128]{2,1,0:T(8,128)(2,1)S(1)} copy-done((bf16[4,32,128]{2,1,0:T(8,128)(2,1)S(1)}, bf16[4,32,128]{2,1,0:T(8,128)(2,1)}, u32[]{:S(2)}) %copy-start.4) | copy-done | bytes 32792
  5.7 27.7 %shard_map.104 = (f32[1,3,4,32,128]{4,3,2,1,0:T(8,128)S(1)}, f32[1,6,4,32,128]{4,3,2,1,0:T(8,128)S(1)}) custom-call(s32[4]{0:T(128)S(1)} %copy-done.5, f32[16,3]{1,0:T(8,128)S(1)} %copy.12.table_ref, s32[16]{0:T(128)S(1)} %copy-done.6, f32[3,4,32,128]{3,2,1,0:T(8,128)S(1)} %copy-done.1, f32[6,4,32,128]{3,2,1,0:T(8,128)S(1)} %copy-done, ...), custom_call_target="tpu_custom_call" | custom-call | tf_op jit(solution)/shard_map/pallas_call | solution.py:466
  33.4 0.7 %copy.15 = f32[1,3,4,32,128]{4,3,2,1,0:T(8,128)} copy(f32[1,3,4,32,128]{4,3,2,1,0:T(8,128)S(1)} %get-tuple-element.4) | data formatting | bytes 393216
  34.1 0.7 %copy.16 = f32[1,6,4,32,128]{4,3,2,1,0:T(8,128)} copy(f32[1,6,4,32,128]{4,3,2,1,0:T(8,128)S(1)} %get-tuple-element.5) | data formatting | bytes 786432
  (1 shorter events, 0.0 us)
Async XLA Ops:
  0.6 1.9 %copy-start.1 = (f32[3,4,32,128]{3,2,1,0:T(8,128)S(1)}, f32[3,4,32,128]{3,2,1,0:T(8,128)}, u32[]{:S(2)}) copy-start(f32[3,4,32,128]{3,2,1,0:T(8,128)} %vel_ref.1) | copy-start | bytes 589828
  2.4 0.8 %copy-start.2 = (bf16[4,32,128]{2,1,0:T(8,128)(2,1)S(1)}, bf16[4,32,128]{2,1,0:T(8,128)(2,1)}, u32[]{:S(2)}) copy-start(bf16[4,32,128]{2,1,0:T(8,128)(2,1)} %lam_ref.1) | copy-start | bytes 98308
  2.4 0.8 %copy-start.5 = (s32[4]{0:T(128)S(1)}, s32[4]{0:T(128)}, u32[]{:S(2)}) copy-start(s32[4]{0:T(128)} %owner_ref.1) | copy-start | bytes 52
  2.5 0.7 %copy-start.6 = (s32[16]{0:T(128)S(1)}, s32[16]{0:T(128)}, u32[]{:S(2)}) copy-start(s32[16]{0:T(128)} %order_ref.1) | copy-start | bytes 196
  3.2 1.0 %copy-start = (f32[6,4,32,128]{3,2,1,0:T(8,128)S(1)}, f32[6,4,32,128]{3,2,1,0:T(8,128)}, u32[]{:S(2)}) copy-start(f32[6,4,32,128]{3,2,1,0:T(8,128)} %sig_ref.1) | copy-start | bytes 1179652
  4.2 0.8 %copy-start.3 = (bf16[4,32,128]{2,1,0:T(8,128)(2,1)S(1)}, bf16[4,32,128]{2,1,0:T(8,128)(2,1)}, u32[]{:S(2)}) copy-start(bf16[4,32,128]{2,1,0:T(8,128)(2,1)} %mu_ref.1) | copy-start | bytes 98308
  5.0 0.8 %copy-start.4 = (bf16[4,32,128]{2,1,0:T(8,128)(2,1)S(1)}, bf16[4,32,128]{2,1,0:T(8,128)(2,1)}, u32[]{:S(2)}) copy-start(bf16[4,32,128]{2,1,0:T(8,128)(2,1)} %buoy_ref.1) | copy-start | bytes 98308

commit v2 on v1

--- a/solution.py
+++ b/solution.py
@@ -8,6 +8,7 @@
 from jax.sharding import PartitionSpec as P
 
 DT = 0.15
+VMEM = 62 * 1024 * 1024
 MESH = pl.DeviceIdType.MESH
 ABOVE = 1
 BELOW = 1
@@ -28,7 +29,7 @@
     lam_ref,
     mu_ref,
     buoy_ref,
-    block_ref,
+    surface_ref,
     vel_out,
     sig_out,
     V,
@@ -36,6 +37,9 @@
     M,
     E,
     raw,
+    raw_rows,
+    tall,
+    packed,
     blocks,
     rows,
     per_step,
@@ -87,11 +91,13 @@
                 barrier, inc=1, device_id=(lax.rem(group + k, groups), upper), device_id_type=MESH
             )
 
+    parts = surface_ref.shape[0] // steps
+    columns = width // groups
     loads = [
         pltpu.make_async_copy(lam_ref, raw.at[0], local_sem.at[0]),
         pltpu.make_async_copy(mu_ref, raw.at[1], local_sem.at[1]),
         pltpu.make_async_copy(buoy_ref, raw.at[2], local_sem.at[2]),
-        pltpu.make_async_copy(block_ref, blocks.at[1, group], local_sem.at[3]),
+        pltpu.make_async_copy(surface_ref, raw_rows, local_sem.at[3]),
         pltpu.make_async_copy(
             vel_ref, V.at[:, pl.ds(own, planes), pl.ds(0, width)], local_sem.at[4]
         ),
@@ -123,13 +129,24 @@
             S[:, n - ABOVE :, TOP:] = jnp.zeros((6, ABOVE, width, depth), jnp.float32)
             M[:, n - ABOVE :] = jnp.zeros((3, ABOVE, width, depth), jnp.float32)
 
+    tall[...] = jnp.zeros_like(tall)
+    loads[3].wait()
+    for t in range(steps):
+        for c in range(parts):
+            at = t * CHUNK + c * planes
+            tall[at : at + planes, :columns] = raw_rows[t * parts + c]
+    for at in range(0, steps * CHUNK, 128):
+        turned = tall[at : at + 128, :].T[:columns]
+        packed[:, at : at + 128] = turned
+        blocks[1, group, :, at : at + 128] = turned
+
     lane = lax.broadcasted_iota(jnp.int32, (width, depth), 1)
     zone = lax.broadcasted_iota(jnp.int32, (planes, width, depth), 2) >= depth // 2
     chosen = order_ref[group]
     for load in loads[:3]:
         load.wait()
     for which in range(3):
-        scale = jnp.where(zone, table_ref[chosen, which] * DT, DT)
+        scale = jnp.where(zone, table_ref[which, chosen] * DT, DT)
         M[which, own : own + planes] = raw[which].astype(jnp.float32) * scale
 
     sides = has_lower.astype(jnp.int32) + has_upper.astype(jnp.int32)
@@ -137,7 +154,7 @@
 
     def block_copy(level, slot, to, index):
         return pltpu.make_async_remote_copy(
-            src_ref=block_ref,
+            src_ref=packed,
             dst_ref=blocks.at[level, slot],
             send_sem=block_send.at[level, index],
             recv_sem=block_recv.at[level, slot],
@@ -206,10 +223,8 @@
             slot = lax.rem(group + k, groups)
             block_copy(level, slot, (slot, to), k).wait_recv()
 
-    loads[3].wait()
     take_blocks(1, slab)
     each_side(lambda: take_blocks(0, lower), lambda: take_blocks(2, upper))
-    columns = width // groups
     for level in range(3):
         for j in range(groups):
             rows[level, j * columns : (j + 1) * columns] = blocks[level, owner_ref[j]]
@@ -228,7 +243,7 @@
             x = i - own
             level = 0 if x < 0 else 2 if x >= planes else 1
             value = per_step[t, level]
-            for c in range(6):
+            for c in range(parts):
                 at = c * planes + x % planes
                 moved = pltpu.roll(value, (source_level - at) % depth, 1)
                 E[t, c, i] = jnp.where(lane == source_level, moved, 0.0)
@@ -387,13 +402,14 @@
     lax.fori_loop(0, steps - 1, one_step, 0)
 
     t = steps - 1
+
     out_copies = []
 
-    def store(ref, out, i, values, sem):
+    def store(ref, out, i, values, kind):
         x = i - own
         for c, value in enumerate(values):
             ref[c, x] = value
-        copy = pltpu.make_async_copy(ref.at[:, x], out.at[0, :, x], out_sem.at[sem, x])
+        copy = pltpu.make_async_copy(ref.at[:, x], out.at[0, :, x], out_sem.at[kind, x])
         copy.start()
         out_copies.append(copy)
 
@@ -434,6 +450,18 @@
 
     each_side(sent_low, sent_high)
     for copy in out_copies:
+        copy.wait()
+
+
+def hand_over(vel_ref, sig_ref, vel_out, sig_out, sem):
+    pairs = [(vel_ref, vel_out, c) for c in range(3)] + [(sig_ref, sig_out, c) for c in range(6)]
+    copies = [
+        pltpu.make_async_copy(src.at[0, c], dst.at[0, c], sem.at[at])
+        for at, (src, dst, c) in enumerate(pairs)
+    ]
+    for copy in copies:
+        copy.start()
+    for copy in copies:
         copy.wait()
 
 
@@ -454,29 +482,30 @@
     steps, parts = surface.shape[:2]
     columns = surface.shape[3]
     n = BELOW + planes + ABOVE
-    packed = surface.transpose(3, 0, 1, 2).reshape(columns, steps, parts * planes)
-    packed = jnp.pad(packed, ((0, 0), (0, 0), (0, CHUNK - parts * planes)))
-    packed = packed.reshape(columns, steps * CHUNK)
     lanes = steps * CHUNK
-    any_space = pl.BlockSpec(memory_space=pl.ANY)
+    far = pl.BlockSpec(memory_space=pl.ANY)
     scalars = pl.BlockSpec(memory_space=pltpu.SMEM)
     f32 = jnp.float32
     message = pltpu.VMEM((steps, 3, width, depth), f32)
     dma = pltpu.SemaphoreType.DMA
-    return pl.pallas_call(
+    shapes = (
+        jax.ShapeDtypeStruct((1, 3, planes, width, depth), f32),
+        jax.ShapeDtypeStruct((1, 6, planes, width, depth), f32),
+    )
+    vel, sig = pl.pallas_call(
         functools.partial(kernel, groups, slabs, steps),
-        out_shape=(
-            jax.ShapeDtypeStruct((1, 3, planes, width, depth), f32),
-            jax.ShapeDtypeStruct((1, 6, planes, width, depth), f32),
-        ),
-        in_specs=[scalars] * 3 + [any_space] * 6,
-        out_specs=(any_space, any_space),
+        out_shape=shapes,
+        in_specs=[scalars] * 3 + [far] * 6,
+        out_specs=(far, far),
         scratch_shapes=[
             pltpu.VMEM((3, n, width + 8, depth), f32),
             pltpu.VMEM((6, n, width + TOP, depth), f32),
             pltpu.VMEM((3, n, width, depth), f32),
             pltpu.VMEM((steps, 6, n, width, depth), f32),
             pltpu.VMEM((3, planes, width, depth), jnp.bfloat16),
+            pltpu.VMEM((steps * parts, planes, columns), f32),
+            pltpu.VMEM((lanes, 128), f32),
+            pltpu.VMEM((columns, lanes), f32),
             pltpu.VMEM((3, groups, columns, lanes), f32),
             pltpu.VMEM((3, width, lanes), f32),
             pltpu.VMEM((steps, 3, width, 128), f32),
@@ -498,19 +527,27 @@
             dma((2, planes)),
         ],
         compiler_params=pltpu.CompilerParams(
-            collective_id=0, has_side_effects=True, vmem_limit_bytes=40 * 1024 * 1024
+            collective_id=0, has_side_effects=True, vmem_limit_bytes=VMEM
         ),
     )(
         block_owner,
-        candidates,
+        candidates.T,
         candidate_of_group,
         velocity,
         stress,
         lame_lambda,
         shear_modulus,
         buoyancy,
-        packed,
+        surface.reshape(steps * parts, planes, columns),
     )
+    return pl.pallas_call(
+        hand_over,
+        out_shape=shapes,
+        in_specs=[far, far],
+        out_specs=(far, far),
+        scratch_shapes=[dma((9,))],
+        compiler_params=pltpu.CompilerParams(vmem_limit_bytes=VMEM),
+    )(vel, sig)
 
 
 def solution(mesh):

time: 35.2 us -> 48.2 us (1.37)
  Pallas kernels: 27.7 us -> 47.4 us
  local copies, waits for them, and re-layouts: 6.46 us -> 0 us
    pallas_call x0 -> x1, Pallas kernels: none -> 19.1 us  [body(): pl.pallas_call(hand_over, out_shape=shapes, in_specs=[far, far], out_spec...]
    unnamed x17 -> x0, local copies, waits for them, and re-layouts: 5.4 us -> none
    reshape x2 -> x0, local copies, waits for them, and re-layouts: 1.05 us -> none  [the longest x1 0.97 us: body(): surface.transpose(3, 0, 1, 2).reshape(columns, steps, parts * planes)]
    pallas_call x1, Pallas kernels: 27.7 us -> 28.3 us  [body(): pl.pallas_call(functools.partial(kernel, groups, slabs, steps), out_shape...]
where the time goes in v2:
time: 48.2 us; the launch traced here: 48 us
  Pallas kernels  47.4 us (98%)
  between operations  0.64 us (1%)
    pallas_call x1, Pallas kernels, body(): pl.pallas_call(functools.partial(kernel, groups, slabs, steps), out_shape...  28.3 us
    pallas_call x1, Pallas kernels, body(): pl.pallas_call(hand_over, out_shape=shapes, in_specs=[far, far], out_spec...  19.1 us

profile of v2, /device:TPU:3, one launch (start us, length us, event | category | flops | bytes accessed | tf_op | source)
XLA Modules:
  0.0 48.0 jit_solution(7333286717902808473)
XLA Ops:
  0.6 28.3 %shard_map.104 = (f32[1,3,4,32,128]{4,3,2,1,0:T(8,128)}, f32[1,6,4,32,128]{4,3,2,1,0:T(8,128)}) custom-call(s32[4]{0:T(128)} %owner_ref.1, f32[3,16]{1,0:T(4,128)} %bitcast.3, s32[16]{0:T(128)} %order_ref.1, f32[3,4,32,128]{3,2,1,0:T(8,128)} %vel_ref.1, f32[6,4,32,128]{3,2,1,0:T(8,128)} %sig_ref.1, bf16[4,32,128]{2,1,0:T(8,128)(2,1)} %lam_ref.1, ...), custom_call_target="tpu_custom_call" | custom-call | tf_op jit(solution)/shard_map/pallas_call | solution.py:495
  29.0 19.1 %shard_map.105 = (f32[1,3,4,32,128]{4,3,2,1,0:T(8,128)}, f32[1,6,4,32,128]{4,3,2,1,0:T(8,128)}) custom-call(f32[1,3,4,32,128]{4,3,2,1,0:T(8,128)} %get-tuple-element.4.vel_ref, f32[1,6,4,32,128]{4,3,2,1,0:T(8,128)} %get-tuple-element.5.sig_ref), custom_call_target="tpu_custom_call" | custom-call | tf_op jit(solution)/shard_map/pallas_call | solution.py:543

commit v3 on v2

--- a/solution.py
+++ b/solution.py
@@ -11,7 +11,7 @@
 VMEM = 62 * 1024 * 1024
 MESH = pl.DeviceIdType.MESH
 ABOVE = 1
-BELOW = 1
+BELOW = 0
 TOP = 8
 CHUNK = 32
 CROSS = (0, 3, 4)
@@ -453,16 +453,24 @@
         copy.wait()
 
 
-def hand_over(vel_ref, sig_ref, vel_out, sig_out, sem):
-    pairs = [(vel_ref, vel_out, c) for c in range(3)] + [(sig_ref, sig_out, c) for c in range(6)]
-    copies = [
-        pltpu.make_async_copy(src.at[0, c], dst.at[0, c], sem.at[at])
-        for at, (src, dst, c) in enumerate(pairs)
+def hand_over(vel_ref, sig_ref, vel_out, sig_out, vel_here, sig_here, load_sem, store_sem):
+    pairs = [(vel_ref, vel_here, vel_out, c) for c in range(3)]
+    pairs += [(sig_ref, sig_here, sig_out, c) for c in range(6)]
+    loads = [
+        pltpu.make_async_copy(src.at[0, c], held.at[c], load_sem.at[at])
+        for at, (src, held, dst, c) in enumerate(pairs)
     ]
-    for copy in copies:
-        copy.start()
-    for copy in copies:
-        copy.wait()
+    stores = [
+        pltpu.make_async_copy(held.at[c], dst.at[0, c], store_sem.at[at])
+        for at, (src, held, dst, c) in enumerate(pairs)
+    ]
+    for load in loads:
+        load.start()
+    for load, store in zip(loads, stores):
+        load.wait()
+        store.start()
+    for store in stores:
+        store.wait()
 
 
 def body(
@@ -545,7 +553,12 @@
         out_shape=shapes,
         in_specs=[far, far],
         out_specs=(far, far),
-        scratch_shapes=[dma((9,))],
+        scratch_shapes=[
+            pltpu.VMEM((3, planes, width, depth), f32),
+            pltpu.VMEM((6, planes, width, depth), f32),
+            dma((9,)),
+            dma((9,)),
+        ],
         compiler_params=pltpu.CompilerParams(vmem_limit_bytes=VMEM),
     )(vel, sig)
 

time: 48.2 us -> 32.8 us (0.68)
  the two profiles are of different devices: /device:TPU:3 before, /device:TPU:4 now
where the time goes in v3:
time: 32.8 us; the launch traced here: 32.5 us
  Pallas kernels  31.9 us (97%)
  between operations  0.64 us (2%)
    pallas_call x1, Pallas kernels, body(): pl.pallas_call(functools.partial(kernel, groups, slabs, steps), out_shape...  30 us
    pallas_call x1, Pallas kernels, body(): pl.pallas_call(hand_over, out_shape=shapes, in_specs=[far, far], out_spec...  1.88 us

profile of v3, /device:TPU:4, one launch (start us, length us, event | category | flops | bytes accessed | tf_op | source)
XLA Modules:
  0.0 32.5 jit_solution(18190432746911188097)
XLA Ops:
  0.6 30.0 %shard_map.104 = (f32[1,3,4,32,128]{4,3,2,1,0:T(8,128)}, f32[1,6,4,32,128]{4,3,2,1,0:T(8,128)}) custom-call(s32[4]{0:T(128)} %owner_ref.1, f32[3,16]{1,0:T(4,128)} %bitcast.3, s32[16]{0:T(128)} %order_ref.1, f32[3,4,32,128]{3,2,1,0:T(8,128)} %vel_ref.1, f32[6,4,32,128]{3,2,1,0:T(8,128)} %sig_ref.1, bf16[4,32,128]{2,1,0:T(8,128)(2,1)} %lam_ref.1, ...), custom_call_target="tpu_custom_call" | custom-call | tf_op jit(solution)/shard_map/pallas_call | solution.py:503
  30.6 1.9 %shard_map.105 = (f32[1,3,4,32,128]{4,3,2,1,0:T(8,128)}, f32[1,6,4,32,128]{4,3,2,1,0:T(8,128)}) custom-call(f32[1,3,4,32,128]{4,3,2,1,0:T(8,128)} %get-tuple-element.4.vel_ref, f32[1,6,4,32,128]{4,3,2,1,0:T(8,128)} %get-tuple-element.5.sig_ref), custom_call_target="tpu_custom_call" | custom-call | tf_op jit(solution)/shard_map/pallas_call | solution.py:551

commit v4 on v3

--- a/solution.py
+++ b/solution.py
@@ -11,7 +11,7 @@
 VMEM = 62 * 1024 * 1024
 MESH = pl.DeviceIdType.MESH
 ABOVE = 1
-BELOW = 0
+BELOW = 1
 TOP = 8
 CHUNK = 32
 CROSS = (0, 3, 4)
@@ -35,12 +35,13 @@
     V,
     S,
     M,
-    E,
     raw,
     raw_rows,
     tall,
     packed,
-    blocks,
+    blocks_low,
+    blocks_own,
+    blocks_high,
     rows,
     per_step,
     down_in,
@@ -60,6 +61,7 @@
     up_recv,
     out_sem,
 ):
+    blocks = (blocks_low, blocks_own, blocks_high)
     planes, width, depth = vel_ref.shape[1:]
     n = BELOW + planes + ABOVE
     own = BELOW
@@ -114,7 +116,7 @@
     @pl.when(jnp.logical_not(has_lower))
     def _():
         up_in[...] = jnp.zeros_like(up_in)
-        blocks[0] = jnp.zeros(blocks.shape[1:], jnp.float32)
+        blocks_low[...] = jnp.zeros_like(blocks_low)
         if BELOW:
             V[:, :BELOW, :width] = jnp.zeros((3, BELOW, width, depth), jnp.float32)
             S[:, :BELOW, TOP:] = jnp.zeros((6, BELOW, width, depth), jnp.float32)
@@ -123,7 +125,7 @@
     @pl.when(jnp.logical_not(has_upper))
     def _():
         down_in[...] = jnp.zeros_like(down_in)
-        blocks[2] = jnp.zeros(blocks.shape[1:], jnp.float32)
+        blocks_high[...] = jnp.zeros_like(blocks_high)
         if ABOVE:
             V[:, n - ABOVE :, :width] = jnp.zeros((3, ABOVE, width, depth), jnp.float32)
             S[:, n - ABOVE :, TOP:] = jnp.zeros((6, ABOVE, width, depth), jnp.float32)
@@ -138,7 +140,7 @@
     for at in range(0, steps * CHUNK, 128):
         turned = tall[at : at + 128, :].T[:columns]
         packed[:, at : at + 128] = turned
-        blocks[1, group, :, at : at + 128] = turned
+        blocks_own[group, :, at : at + 128] = turned
 
     lane = lax.broadcasted_iota(jnp.int32, (width, depth), 1)
     zone = lax.broadcasted_iota(jnp.int32, (planes, width, depth), 2) >= depth // 2
@@ -155,7 +157,7 @@
     def block_copy(level, slot, to, index):
         return pltpu.make_async_remote_copy(
             src_ref=packed,
-            dst_ref=blocks.at[level, slot],
+            dst_ref=blocks[level].at[slot],
             send_sem=block_send.at[level, index],
             recv_sem=block_recv.at[level, slot],
             device_id=to,
@@ -223,46 +225,48 @@
             slot = lax.rem(group + k, groups)
             block_copy(level, slot, (slot, to), k).wait_recv()
 
-    take_blocks(1, slab)
-    each_side(lambda: take_blocks(0, lower), lambda: take_blocks(2, upper))
-    for level in range(3):
+    halves = 128 // CHUNK
+
+    def prepare(level):
         for j in range(groups):
-            rows[level, j * columns : (j + 1) * columns] = blocks[level, owner_ref[j]]
-    halves = 128 // CHUNK
-    for t in range(steps):
-        at = 128 * (t // halves)
-        for level in range(3):
+            rows[level, j * columns : (j + 1) * columns] = blocks[level][owner_ref[j]]
+        for t in range(steps):
+            at = 128 * (t // halves)
             piece = rows[level, :, at : at + 128]
             shift = (t % halves) * CHUNK
             per_step[t, level] = pltpu.roll(piece, 128 - shift, 1) if shift else piece
 
+    take_blocks(1, slab)
+    prepare(1)
     source_level = depth // 8
 
-    def spread(t, carry):
-        for i in range(n):
-            x = i - own
-            level = 0 if x < 0 else 2 if x >= planes else 1
-            value = per_step[t, level]
-            for c in range(parts):
-                at = c * planes + x % planes
-                moved = pltpu.roll(value, (source_level - at) % depth, 1)
-                E[t, c, i] = jnp.where(lane == source_level, moved, 0.0)
-        return carry
-
-    lax.fori_loop(0, steps, spread, 0)
+    def pulse(t, c, i):
+        x = i - own
+        level = 0 if x < 0 else 2 if x >= planes else 1
+        at = c * planes + x % planes
+        moved = pltpu.roll(per_step[t, level], (source_level - at) % depth, 1)
+        return jnp.where(lane == source_level, moved, 0.0)
 
     for load in loads[4:]:
         load.wait()
 
-    def ghosts_here():
-        for copy in ghost_copies(True):
-            copy.wait_recv()
-
-    def ghosts_below_here():
-        for copy in ghost_copies(False):
-            copy.wait_recv()
-
-    each_side(ghosts_below_here, ghosts_here)
+    def arrive_top():
+        @pl.when(has_upper)
+        def _():
+            for copy in ghost_copies(True):
+                copy.wait_recv()
+            take_blocks(2, upper)
+
+        prepare(2)
+
+    def arrive_bottom():
+        @pl.when(has_lower)
+        def _():
+            for copy in ghost_copies(False):
+                copy.wait_recv()
+            take_blocks(0, lower)
+
+        prepare(0)
 
     def before(f):
         return jnp.where(lane == 0, 0.0, pltpu.roll(f, 1, 1))
@@ -283,9 +287,9 @@
             west = [here(c, i - 1) for c in CROSS]
         sxx, syy, szz, sxy, sxz, syz = (here(c, i) for c in range(6))
         b = M[2, i]
-        ax = (sxx - west[0]) + (sxy - south(3, i)) + (sxz - before(sxz)) + E[t, 0, i]
-        ay = (sxy - west[1]) + (syy - south(1, i)) + (syz - before(syz)) + E[t, 1, i]
-        az = (sxz - west[2]) + (syz - south(5, i)) + (szz - before(szz)) + E[t, 2, i]
+        ax = (sxx - west[0]) + (sxy - south(3, i)) + (sxz - before(sxz)) + pulse(t, 0, i)
+        ay = (sxy - west[1]) + (syy - south(1, i)) + (syz - before(syz)) + pulse(t, 1, i)
+        az = (sxz - west[2]) + (syz - south(5, i)) + (szz - before(szz)) + pulse(t, 2, i)
         return [V[c, i, :width] + b * a for c, a in enumerate((ax, ay, az))]
 
     def new_sig(i, t):
@@ -298,15 +302,15 @@
         lam, mu = M[0, i], M[1, i]
         mu2 = mu + mu
         xx, yy, zz = ex - vx, ny - vy, after(vz) - vz
-        zz_in = E[t, 5, i]
+        zz_in = pulse(t, 5, i)
         spread_all = lam * (xx + yy + zz)
         return [
             here(0, i) + (spread_all + mu2 * xx),
             here(1, i) + (spread_all + mu2 * yy),
             here(2, i) + (spread_all + mu2 * zz + (lam + mu2) * zz_in),
             here(3, i) + mu * ((nx - vx) + (ey - vy)),
-            here(4, i) + mu * ((after(vx) - vx) + (ez - vz) + E[t, 3, i]),
-            here(5, i) + mu * ((after(vy) - vy) + (nz - vz) + E[t, 4, i]),
+            here(4, i) + mu * ((after(vx) - vx) + (ez - vz) + pulse(t, 3, i)),
+            here(5, i) + mu * ((after(vy) - vy) + (nz - vz) + pulse(t, 4, i)),
         ]
 
     def set_vel(i, t):
@@ -376,18 +380,21 @@
                     set_vel(i, t)
                     done.append(i)
             send_up(t)
-        for i in range(1, n - 1):
+        for i in range(own + 1, own + planes):
             if i not in done:
                 set_vel(i, t)
 
+        pl.when(t == 0)(arrive_top)
+
         @pl.when(t > 0)
         def _():
             finish_top(t)
 
-        set_vel(n - 1, t)
+        for i in range(own + planes, n):
+            set_vel(i, t)
         if not early:
             send_up(t)
-        for i in range(n - 2, 0, -1):
+        for i in range(n - 2, own, -1):
             if i != uplane:
                 set_sig(i, t)
 
@@ -395,8 +402,11 @@
         def _():
             up_copy(t - 1).wait_recv()
 
-        set_vel(0, t)
-        set_sig(0, t)
+        pl.when(t == 0)(arrive_bottom)
+        for i in range(own, -1, -1):
+            set_vel(i, t)
+        for i in range(own, -1, -1):
+            set_sig(i, t)
         return carry
 
     lax.fori_loop(0, steps - 1, one_step, 0)
@@ -509,12 +519,13 @@
             pltpu.VMEM((3, n, width + 8, depth), f32),
             pltpu.VMEM((6, n, width + TOP, depth), f32),
             pltpu.VMEM((3, n, width, depth), f32),
-            pltpu.VMEM((steps, 6, n, width, depth), f32),
             pltpu.VMEM((3, planes, width, depth), jnp.bfloat16),
             pltpu.VMEM((steps * parts, planes, columns), f32),
             pltpu.VMEM((lanes, 128), f32),
             pltpu.VMEM((columns, lanes), f32),
-            pltpu.VMEM((3, groups, columns, lanes), f32),
+            pltpu.VMEM((groups, columns, lanes), f32),
+            pltpu.VMEM((groups, columns, lanes), f32),
+            pltpu.VMEM((groups, columns, lanes), f32),
             pltpu.VMEM((3, width, lanes), f32),
             pltpu.VMEM((steps, 3, width, 128), f32),
             message,

time: 32.8 us -> 29.8 us (0.909)
  the two profiles are of different devices: /device:TPU:4 before, /device:TPU:3 now
where the time goes in v4:
time: 29.8 us; the launch traced here: 29.6 us
  Pallas kernels  29 us (97%)
  between operations  0.64 us (2%)
    pallas_call x1, Pallas kernels, body(): pl.pallas_call(functools.partial(kernel, groups, slabs, steps), out_shape...  27.1 us
    pallas_call x1, Pallas kernels, body(): pl.pallas_call(hand_over, out_shape=shapes, in_specs=[far, far], out_spec...  1.88 us

profile of v4, /device:TPU:3, one launch (start us, length us, event | category | flops | bytes accessed | tf_op | source)
XLA Modules:
  0.0 29.6 jit_solution(2809090611163823111)
XLA Ops:
  0.6 27.1 %shard_map.104 = (f32[1,3,4,32,128]{4,3,2,1,0:T(8,128)}, f32[1,6,4,32,128]{4,3,2,1,0:T(8,128)}) custom-call(s32[4]{0:T(128)} %owner_ref.1, f32[3,16]{1,0:T(4,128)} %bitcast.3, s32[16]{0:T(128)} %order_ref.1, f32[3,4,32,128]{3,2,1,0:T(8,128)} %vel_ref.1, f32[6,4,32,128]{3,2,1,0:T(8,128)} %sig_ref.1, bf16[4,32,128]{2,1,0:T(8,128)(2,1)} %lam_ref.1, ...), custom_call_target="tpu_custom_call" | custom-call | tf_op jit(solution)/shard_map/pallas_call | solution.py:513
  27.7 1.9 %shard_map.105 = (f32[1,3,4,32,128]{4,3,2,1,0:T(8,128)}, f32[1,6,4,32,128]{4,3,2,1,0:T(8,128)}) custom-call(f32[1,3,4,32,128]{4,3,2,1,0:T(8,128)} %get-tuple-element.4.vel_ref, f32[1,6,4,32,128]{4,3,2,1,0:T(8,128)} %get-tuple-element.5.sig_ref), custom_call_target="tpu_custom_call" | custom-call | tf_op jit(solution)/shard_map/pallas_call | solution.py:562

commit v5 on v4

--- a/solution.py
+++ b/solution.py
@@ -48,6 +48,7 @@
     up_in,
     down_out,
     up_out,
+    first_out,
     vel_last,
     sig_last,
     local_sem,
@@ -165,24 +166,16 @@
         )
 
     def ghost_copies(down):
-        count, to = (ABOVE, lower) if down else (BELOW, upper)
+        to = lower if down else upper
         base = 0 if down else 3
-        source = 0 if down else planes - BELOW
-        target = own + planes if down else 0
-        pairs = []
-        if count:
-            there = pl.ds(target, count)
-            pairs = [
-                (sig_ref.at[:, pl.ds(source, count)], S.at[:, there, pl.ds(TOP, width)]),
-                (vel_ref.at[:, pl.ds(source, count)], V.at[:, there, pl.ds(0, width)]),
-                (M.at[:, pl.ds(own + source, count)], M.at[:, there]),
-            ]
-        else:
-            base = 3
-        if not down:
-            edge = planes - 1 - BELOW
-            pairs.append((sig_ref.at[0, edge], up_in.at[0, 0]))
-            pairs.append((sig_ref.at[pl.ds(3, 2), edge], up_in.at[0, pl.ds(1, 2)]))
+        edge = 0 if down else planes - 1
+        there = n - 1 if down else 0
+        pairs = [
+            (sig_ref.at[:, edge], S.at[:, there, pl.ds(TOP, width)]),
+            (M.at[:, own + edge], M.at[:, there]),
+        ]
+        if down:
+            pairs.append((vel_ref.at[:, edge], V.at[:, there, pl.ds(0, width)]))
         return [
             pltpu.make_async_remote_copy(
                 src_ref=src,
@@ -195,6 +188,16 @@
             for at, (src, dst) in enumerate(pairs)
         ]
 
+    def first_copy():
+        return pltpu.make_async_remote_copy(
+            src_ref=first_out,
+            dst_ref=V.at[:, 0, pl.ds(0, width)],
+            send_sem=ghost_send.at[5],
+            recv_sem=ghost_recv.at[5],
+            device_id=(group, upper),
+            device_id_type=MESH,
+        )
+
     def level_slots(level):
         return range(1 if level == 1 else 0, groups)
 
@@ -265,6 +268,7 @@
             for copy in ghost_copies(False):
                 copy.wait_recv()
             take_blocks(0, lower)
+            first_copy().wait_recv()
 
         prepare(0)
 
@@ -372,7 +376,15 @@
                 down_out[t, c] = values[c]
             down_copy(t).start()
 
-        done = [dplane]
+        done = [dplane, own + planes - 1]
+        values = set_vel(own + planes - 1, t)
+
+        @pl.when(jnp.logical_and(has_upper, t == 0))
+        def _():
+            for c in range(3):
+                first_out[c] = values[c]
+            first_copy().start()
+
         early = uplane + 1 <= n - 2
         if early:
             for i in (uplane, uplane + 1):
@@ -403,8 +415,12 @@
             up_copy(t - 1).wait_recv()
 
         pl.when(t == 0)(arrive_bottom)
-        for i in range(own, -1, -1):
-            set_vel(i, t)
+        set_vel(own, t)
+
+        @pl.when(t > 0)
+        def _():
+            set_vel(0, t)
+
         for i in range(own, -1, -1):
             set_sig(i, t)
         return carry
@@ -455,6 +471,7 @@
             block_copy(0, group, (lax.rem(group + k, groups), upper), k).wait_send()
         for copy in ghost_copies(False):
             copy.wait_send()
+        first_copy().wait_send()
         for s in range(last_up + 1):
             up_copy(s).wait_send()
 
@@ -532,13 +549,14 @@
             message,
             message,
             message,
+            pltpu.VMEM((3, width, depth), f32),
             pltpu.VMEM((3, planes, width, depth), f32),
             pltpu.VMEM((6, planes, width, depth), f32),
             dma((6,)),
             dma((3, groups)),
             dma((3, groups)),
-            dma((8,)),
-            dma((8,)),
+            dma((6,)),
+            dma((6,)),
             dma((steps,)),
             dma((steps,)),
             dma((steps,)),

time: 29.8 us -> 29.5 us (0.990)
  Pallas kernels: 29 us -> 28.6 us
    pallas_call x1, Pallas kernels: 27.1 us -> 26.7 us  [body(): pl.pallas_call(functools.partial(kernel, groups, slabs, steps), out_shape...]
where the time goes in v5:
time: 29.5 us; the launch traced here: 29.3 us
  Pallas kernels  28.6 us (97%)
  between operations  0.64 us (2%)
    pallas_call x1, Pallas kernels, body(): pl.pallas_call(functools.partial(kernel, groups, slabs, steps), out_shape...  26.7 us
    pallas_call x1, Pallas kernels, body(): pl.pallas_call(hand_over, out_shape=shapes, in_specs=[far, far], out_spec...  1.88 us

profile of v5, /device:TPU:3, one launch (start us, length us, event | category | flops | bytes accessed | tf_op | source)
XLA Modules:
  0.0 29.3 jit_solution(1795024407901423941)
XLA Ops:
  0.6 26.7 %shard_map.104 = (f32[1,3,4,32,128]{4,3,2,1,0:T(8,128)}, f32[1,6,4,32,128]{4,3,2,1,0:T(8,128)}) custom-call(s32[4]{0:T(128)} %owner_ref.1, f32[3,16]{1,0:T(4,128)} %bitcast.3, s32[16]{0:T(128)} %order_ref.1, f32[3,4,32,128]{3,2,1,0:T(8,128)} %vel_ref.1, f32[6,4,32,128]{3,2,1,0:T(8,128)} %sig_ref.1, bf16[4,32,128]{2,1,0:T(8,128)(2,1)} %lam_ref.1, ...), custom_call_target="tpu_custom_call" | custom-call | tf_op jit(solution)/shard_map/pallas_call | solution.py:530
  27.4 1.9 %shard_map.105 = (f32[1,3,4,32,128]{4,3,2,1,0:T(8,128)}, f32[1,6,4,32,128]{4,3,2,1,0:T(8,128)}) custom-call(f32[1,3,4,32,128]{4,3,2,1,0:T(8,128)} %get-tuple-element.4.vel_ref, f32[1,6,4,32,128]{4,3,2,1,0:T(8,128)} %get-tuple-element.5.sig_ref), custom_call_target="tpu_custom_call" | custom-call | tf_op jit(solution)/shard_map/pallas_call | solution.py:580
